TPU v7x, 32 devices: a whole 2x2x4 slice. The times are simulated.
32 devices in a mesh: pp: 4 (over y, x), cp: 4 (over z), dp: 2 (over core).
Axes of the slice: x: 2, y: 2, z: 4, core: 2. Of those that a mesh axis runs over, the one named last changes fastest.
Arguments:
- queries: bfloat16 [4, 512, 1024], P('pp', 'cp', 'dp'), may hold values from -8 to 8
- keys: bfloat16 [4, 512, 128], P('pp', 'cp'), may hold values from -8 to 8
- values: bfloat16 [4, 512, 128], P('pp', 'cp'), may hold values from -6 to 6
- grad_out: bfloat16 [4, 512, 1024], P('pp', 'cp', 'dp'), may hold values from -6 to 6
- span_order: int32 [8], replicated, may hold values from 0 to 7, each once
Outputs:
- attn_out: bfloat16 [4, 512, 1024], P('pp', 'cp', 'dp')
- grad_queries: bfloat16 [4, 512, 1024], P('pp', 'cp', 'dp')
- grad_keys: bfloat16 [4, 512, 128], P('pp', 'cp')
- grad_values: bfloat16 [4, 512, 128], P('pp', 'cp')
Inputs may be any that keep to these rules, and one draw needn't show every extreme that they name: Every block number appears once; the rows of index c of cp hold blocks span_order[2c] and span_order[2c + 1].
All inputs are finite; a program needn't handle non-finite values.
Results may differ from a plain program's by a relative error of at most 0.038.
Values may be sent and summed in bfloat16 or wider, within the bound.
A program may use at most 64 MiB of HBM per device.

v0:
```python
import math

import jax
import jax.numpy as jnp
from jax import lax
from jax.sharding import PartitionSpec as P


def shifted(block, axis, distance):
    devices = range(lax.axis_size(axis))
    route = [((i - distance) % len(devices), i) for i in devices]
    return lax.ppermute(block, axis, route)


def body(queries, keys, values, grad_out, span_order):
    query_rows = queries[0]
    tok_rows = query_rows.shape[0]
    head_dim = keys.shape[2]
    head_count = query_rows.shape[1] // head_dim
    half_len = tok_rows // 2
    own_rank = lax.axis_index("cp")
    context_size = lax.axis_size("cp")
    all_rows = tok_rows * context_size
    score_scale = 1.0 / math.sqrt(head_dim)
    offsets = jnp.arange(half_len, dtype=jnp.int32)
    own_ids = lax.dynamic_slice_in_dim(span_order, own_rank * 2, 2)
    query_pos = (own_ids[:, None] * half_len + offsets[None, :]).reshape(tok_rows)
    key_pos = (span_order[:, None] * half_len + offsets[None, :]).reshape(all_rows)
    incoming = shifted(grad_out, "pp", -1)[0]
    key_all, value_all = (
        lax.all_gather(keys[0], "cp", axis=0, tiled=True),
        lax.all_gather(values[0], "cp", axis=0, tiled=True),
    )
    key_block = math.gcd(all_rows, 512)
    block_count = all_rows // key_block
    key_pieces = key_all.reshape(block_count, key_block, head_dim)
    value_pieces = value_all.reshape(block_count, key_block, head_dim)
    pos_pieces = key_pos.reshape(block_count, key_block)
    query_heads = query_rows.reshape(tok_rows, head_count, head_dim)
    grad_heads = incoming.reshape(tok_rows, head_count, head_dim)

    def forward_step(state_in, pieces):
        run_peak, run_total, out_accum = state_in
        key_piece, value_piece, pos_piece = pieces
        scores = (
            jnp.einsum("thd,kd->thk", query_heads, key_piece, preferred_element_type=jnp.float32)
            * score_scale
        )
        visible = pos_piece[None, None, :] <= query_pos[:, None, None]
        scores = jnp.where(visible, scores, -1e30)
        new_peak = jnp.maximum(run_peak, jnp.max(scores, axis=2))
        weights = jnp.where(visible, jnp.exp(scores - new_peak[:, :, None]), 0.0)
        factor = jnp.exp(run_peak - new_peak)
        run_total = run_total * factor + jnp.sum(weights, axis=2)
        out_accum = out_accum * factor[:, :, None] + jnp.einsum(
            "thk,kd->thd",
            weights.astype(jnp.bfloat16),
            value_piece,
            preferred_element_type=jnp.float32,
        )
        return ((new_peak, run_total, out_accum), None)

    start_state = (
        jnp.full((tok_rows, head_count), -1e30, jnp.float32),
        jnp.zeros((tok_rows, head_count), jnp.float32),
        jnp.zeros((tok_rows, head_count, head_dim), jnp.float32),
    )
    (run_peak, run_total, out_accum), unused = lax.scan(
        forward_step, start_state, (key_pieces, value_pieces, pos_pieces)
    )
    attended = (out_accum / run_total[:, :, None]).astype(jnp.bfloat16)
    log_total = run_peak + jnp.log(run_total)
    row_dots = jnp.sum(grad_heads.astype(jnp.float32) * attended.astype(jnp.float32), axis=2)

    def backward_step(grad_query, pieces):
        key_piece, value_piece, pos_piece = pieces
        scores = (
            jnp.einsum("thd,kd->thk", query_heads, key_piece, preferred_element_type=jnp.float32)
            * score_scale
        )
        visible = pos_piece[None, None, :] <= query_pos[:, None, None]
        attn_prob = jnp.where(visible, jnp.exp(scores - log_total[:, :, None]), 0.0)
        grad_prob = jnp.einsum(
            "thd,kd->thk", grad_heads, value_piece, preferred_element_type=jnp.float32
        )
        dscore = (attn_prob * (grad_prob - row_dots[:, :, None])).astype(jnp.bfloat16)
        grad_query = grad_query + jnp.einsum(
            "thk,kd->thd", dscore, key_piece, preferred_element_type=jnp.float32
        )
        grad_key = (
            jnp.einsum("thk,thd->kd", dscore, query_heads, preferred_element_type=jnp.float32)
            * score_scale
        )
        grad_value = jnp.einsum(
            "thk,thd->kd",
            attn_prob.astype(jnp.bfloat16),
            grad_heads,
            preferred_element_type=jnp.float32,
        )
        return (grad_query, jnp.concatenate([grad_key, grad_value], axis=1))

    grad_query, pieces_out = lax.scan(
        backward_step,
        jnp.zeros((tok_rows, head_count, head_dim), jnp.float32),
        (key_pieces, value_pieces, pos_pieces),
    )
    grad_query = (
        (grad_query * score_scale).astype(jnp.bfloat16).reshape(tok_rows, head_count * head_dim)
    )
    partial_value = pieces_out.reshape(all_rows, 2 * head_dim)
    shared_rows = lax.psum_scatter(partial_value, "cp", scatter_dimension=0, tiled=True)
    summed = lax.psum(shared_rows, "dp").astype(jnp.bfloat16)
    attn_rows = attended.reshape(tok_rows, head_count * head_dim)
    return (
        attn_rows[None],
        grad_query[None],
        summed[None, :, :head_dim],
        summed[None, :, head_dim:],
    )


def solution(mesh):
    in_specs = (
        P("pp", "cp", "dp"),
        P("pp", "cp", None),
        P("pp", "cp", None),
        P("pp", "cp", "dp"),
        P(),
    )
    out_specs = (P("pp", "cp", "dp"), P("pp", "cp", "dp"), P("pp", "cp", None), P("pp", "cp", None))
    return jax.shard_map(body, mesh=mesh, in_specs=in_specs, out_specs=out_specs, check_vma=False)
```

profile of v0, /device:TPU:0, one launch (start us, length us, event | category | flops | bytes accessed | tf_op | source)
XLA Modules:
  0.0 75.6 jit_solution(576384811044222357)
XLA Ops:
  7.2 0.0 copy-start.2
  7.2 0.0 reduce-scatter.2.cloned.1.call-start
  7.2 3.9 %collective-permute-start = (bf16[1,128,512]{2,1,0:T(8,128)(2,1)}, bf16[1,128,512]{2,1,0:T(8,128)(2,1)S(1)}, u32[]{:S(2)}, u32[]{:S(2)}) collective-permute-start(bf16[1,128,512]{2,1,0:T(8,128)(2,1)} %param.8), channel_id=1, source_target_pairs={{8,0},{16,8},{24,16},{0,24},{9,1},{17,9},{25,17},{1,25},{10,2},{18... | collective-permute-start | bytes 393224 | tf_op jit(solution)/shard_map/ppermute | solution.py:12
  11.2 0.0 copy-done.2
  11.2 0.1 iota_add_fusion
  11.2 0.1 add.78
  11.3 0.1 dynamic-slice_multiply_fusion
  11.4 0.1 iota_add_fusion.1
  11.5 0.1 add.83
  11.6 0.0 copy-start
  11.6 1.0 %copy.25 = bf16[1,128,512]{1,2,0:T(8,128)(2,1)S(1)} copy(bf16[1,128,512]{2,1,0:T(8,128)(2,1)} %param.5) | data formatting | bytes 262144 | tf_op jit(solution)/shard_map/reshape;squeeze | solution.py:39
  12.6 0.0 copy-done
  12.6 13.6 %all-gather = bf16[1,512,128]{2,1,0:T(8,128)(2,1)S(1)} all-gather(bf16[1,128,128]{2,1,0:T(8,128)(2,1)S(1)} %copy-done), channel_id=2, replica_groups=mesh['pp'=4,'cp'=4,'dp'=2] {'cp'}, dimensions={1}, use_global_device_ids=true | all-gather | bytes 163840 | tf_op jit(solution)/shard_map/all_gather | solution.py:31
  26.2 0.1 broadcast_compare_fusion
  26.4 0.4 select_reduce_fusion
  26.8 0.0 copy-start.1
  26.8 0.4 fusion.7
  27.2 0.4 copy-done.1
  27.6 0.1 copy.10
  27.7 12.3 %all-gather.1 = bf16[1,512,128]{1,2,0:T(8,128)(2,1)S(1)} all-gather(bf16[1,128,128]{1,2,0:T(8,128)(2,1)S(1)} %copy.10), channel_id=3, replica_groups=mesh['pp'=4,'cp'=4,'dp'=2] {'cp'}, dimensions={1}, use_global_device_ids=true | all-gather | bytes 163840 | tf_op jit(solution)/shard_map/all_gather | solution.py:32
  39.9 0.0 collective-permute-done
  39.9 0.1 copy.11
  40.0 0.4 convolution_bitcast_fusion
  40.5 0.5 multiply_reduce_fusion
  41.0 0.4 fusion.1
  41.4 0.2 fusion.2
  41.7 0.8 %pad_maximum_fusion = f32[512,256]{0,1:T(8,128)} fusion(f32[512,128]{0,1:T(8,128)S(1)} %convolution_bitcast_fusion, f32[512,128]{0,1:T(8,128)S(1)} %fusion.2), kind=kLoop, calls=%fused_computation.18 | loop fusion | flops 131072 | bytes 1048576 | tf_op jit(solution)/shard_map/while/body/eval_jaxpr/concatenate | solution.py:100
  42.5 0.0 reduce-scatter.2.cloned.1.call-update
  42.5 0.8 %copy.16 = bf16[1,128,512]{2,1,0:T(8,128)(2,1)} copy(bf16[1,128,512]{1,2,0:T(8,128)(2,1)S(1)} %bitcast.46) | data formatting | bytes 262144
  43.3 0.3 fusion.4
  43.6 0.8 %copy.17 = bf16[1,128,512]{2,1,0:T(8,128)(2,1)} copy(bf16[1,128,512]{1,2,0:T(8,128)(2,1)S(1)} %bitcast.45) | data formatting | bytes 262144
  44.4 18.4 %reduce-scatter.2.cloned.1.call-done = f32[128,256]{0,1:T(8,128)} async-done(((f32[512,256]{0,1:T(8,128)}), f32[128,256]{0,1:T(8,128)}) %reduce-scatter.2.cloned.1.call-update) | async-done | bytes 131088 | tf_op jit(solution)/shard_map/reduce_scatter | solution.py:111
  62.8 4.5 %all-reduce.1 = bf16[128,256]{0,1:T(8,128)(2,1)S(1)} all-reduce(f32[128,256]{0,1:T(8,128)} %reduce-scatter.2.cloned.1.call-done), channel_id=1, replica_groups=mesh['pp'=4,'cp'=4,'dp'=2] {'dp'}, use_global_device_ids=true, to_apply=%region_4.5 | all-reduce | flops 32768 | bytes 196608 | tf_op jit(solution)/shard_map/psum | solution.py:112
  67.3 0.7 copy.18
  68.0 0.7 copy.19
  (4 shorter events, 0.0 us)
Async XLA Ops:
  7.2 4.0 %copy-start.2 = (s32[8]{0:T(128)S(1)}, s32[8]{0:T(128)}, u32[]{:S(2)}) copy-start(s32[8]{0:T(128)} %param.9) | copy-start | bytes 100
  7.2 55.6 %reduce-scatter.2.cloned.1.call-start = ((), (), s32[]{:S(2)}) async-start(), calls=%async_computation.1 | async-start | bytes 655360 | tf_op jit(solution)/shard_map/reduce_scatter | solution.py:111
  7.2 32.7 %collective-permute-start = (bf16[1,128,512]{2,1,0:T(8,128)(2,1)}, bf16[1,128,512]{2,1,0:T(8,128)(2,1)S(1)}, u32[]{:S(2)}, u32[]{:S(2)}) collective-permute-start(bf16[1,128,512]{2,1,0:T(8,128)(2,1)} %param.8), channel_id=1, source_target_pairs={{8,0},{16,8},{24,16},{0,24},{9,1},{17,9},{25,17},{1,25},{10,2},{18... | collective-permute-start | bytes 393224 | tf_op jit(solution)/shard_map/ppermute | solution.py:12
  11.6 1.0 %copy-start = (bf16[1,128,128]{2,1,0:T(8,128)(2,1)S(1)}, bf16[1,128,128]{2,1,0:T(8,128)(2,1)}, u32[]{:S(2)}) copy-start(bf16[1,128,128]{2,1,0:T(8,128)(2,1)} %param.6) | copy-start | bytes 98308
  26.8 0.8 %copy-start.1 = (bf16[1,128,128]{2,1,0:T(8,128)(2,1)S(1)}, bf16[1,128,128]{2,1,0:T(8,128)(2,1)}, u32[]{:S(2)}) copy-start(bf16[1,128,128]{2,1,0:T(8,128)(2,1)} %param.7) | copy-start | bytes 98308
Sparse Core Ops, SparseCore 0:
  42.6 20.0 reduce-scatter.1
where the time goes:
time: 75.9 us; the launch traced here: 75.6 us
  blocking collectives  30.4 us (40%)
  waiting for transfers between devices  18.4 us (24%)
  between operations  14.1 us (19%)
  local copies, waits for them, and re-layouts  4.79 us (6%)
  starting transfers between devices  3.98 us (5%)
  matrix products  2.31 us (3%)
  other arithmetic  1.54 us (2%)
    reduce_scatter x1, waiting for transfers between devices, body(): lax.psum_scatter(partial_value, 'cp', scatter_dimension=0, tiled=True)  18.4 us
    all_gather x1, blocking collectives, body(): lax.all_gather(keys[0], 'cp', axis=0, tiled=True)  13.6 us
    all_gather x1, blocking collectives, body(): lax.all_gather(values[0], 'cp', axis=0, tiled=True)  12.3 us
    psum x1, blocking collectives, body(): summed = lax.psum(shared_rows, 'dp').astype(jnp.bfloat16)  4.52 us
    ppermute x1, starting transfers between devices, shifted(): return lax.ppermute(block, axis, route)  3.95 us
    unnamed x11, local copies, waits for them, and re-layouts  3.47 us
  transfers between devices with their start and end apart: 2, of which 1 were waited for; matrix products, arithmetic and copies ran while one was open for 6% of the time, Pallas kernels for 0%

commit v1 on v0

v1 whole, which is shorter than its diff:
```python
import functools
import math

import jax
import jax.numpy as jnp
from jax import lax
from jax.experimental import pallas as pl
from jax.experimental.pallas import tpu as pltpu
from jax.sharding import PartitionSpec as P

MESH = pl.DeviceIdType.MESH
NEG = -1e30


def each(count, fn):
    if count <= 8:
        for i in range(count):
            fn(i)
    else:

        def step(i, carry):
            fn(i)
            return carry

        lax.fori_loop(0, count, step, 0)


def kernel(
    n_pp, n, n_dp, heads, span_ref, q_ref, k_ref, v_ref, g_ref,
    o_ref, dq_ref, dk_ref, dv_ref,
    kv, qg, wts, dprob, stat, pair, xsend, xrecv, rsend, rrecv, own, fin, ovm, dqvm,
    q_sem, kv_sem, out_sem, g_send, g_recv, s_send, s_recv, f_send, f_recv,
    x_send, x_recv, r_send, r_recv, e_send, e_recv,
):
    tok, dh = kv.shape[2], kv.shape[3]
    half = tok // 2
    width = heads * dh if False else heads * tok
    scale = 1.0 / math.sqrt(dh)
    f32, bf16 = jnp.float32, jnp.bfloat16
    s = lax.axis_index("pp")
    c = lax.axis_index("cp")
    d = lax.axis_index("dp")
    other = 1 - d
    before = lax.rem(s + n_pp - 1, n_pp)
    after = lax.rem(s + 1, n_pp)

    def peer(i):
        return lax.rem(c + i, n)

    barrier = pltpu.get_barrier_semaphore()
    pl.semaphore_signal(barrier, inc=1, device_id={"pp": before}, device_id_type=MESH)
    pl.semaphore_signal(barrier, inc=1, device_id={"pp": after}, device_id_type=MESH)
    pl.semaphore_signal(barrier, inc=1, device_id={"dp": other}, device_id_type=MESH)
    each(
        n - 1,
        lambda i: pl.semaphore_signal(
            barrier, inc=1, device_id={"cp": peer(i + 1)}, device_id_type=MESH
        ),
    )

    load_k = pltpu.make_async_copy(k_ref.at[0], kv.at[0, c], kv_sem.at[0])
    load_v = pltpu.make_async_copy(v_ref.at[0], kv.at[1, c], kv_sem.at[1])
    load_k.start()
    load_v.start()
    load_q = [
        pltpu.make_async_copy(
            q_ref.at[0, :, pl.ds(h * dh, dh)], qg.at[0, pl.ds(h * tok, tok), :], q_sem.at[h]
        )
        for h in range(heads)
    ]
    for copy in load_q:
        copy.start()
    load_k.wait()
    load_v.wait()

    pl.semaphore_wait(barrier, n + 2)

    def spread(i):
        return pltpu.make_async_remote_copy(
            src_ref=kv.at[d, c], dst_ref=kv.at[d, c],
            send_sem=s_send.at[i], recv_sem=s_recv.at[c],
            device_id={"cp": peer(i)}, device_id_type=MESH,
        )

    def arrive(i):
        j = peer(i)
        return pltpu.make_async_remote_copy(
            src_ref=kv.at[d, j], dst_ref=kv.at[d, j],
            send_sem=s_send.at[i], recv_sem=s_recv.at[j],
            device_id={"cp": j}, device_id_type=MESH,
        )

    def forward(i):
        j = peer(i)
        return pltpu.make_async_remote_copy(
            src_ref=kv.at[d, j], dst_ref=kv.at[d, j],
            send_sem=f_send.at[i], recv_sem=f_recv.at[j],
            device_id={"dp": other}, device_id_type=MESH,
        )

    def forwarded(i):
        j = peer(i)
        return pltpu.make_async_remote_copy(
            src_ref=kv.at[other, j], dst_ref=kv.at[other, j],
            send_sem=f_send.at[i], recv_sem=f_recv.at[j],
            device_id={"dp": other}, device_id_type=MESH,
        )

    each(n - 1, lambda i: spread(i + 1).start())
    shift = [
        pltpu.make_async_remote_copy(
            src_ref=g_ref.at[0, :, pl.ds(h * dh, dh)],
            dst_ref=qg.at[1, pl.ds(h * tok, tok), :],
            send_sem=g_send.at[h], recv_sem=g_recv.at[h],
            device_id={"pp": before}, device_id_type=MESH,
        )
        for h in range(heads)
    ]
    for copy in shift:
        copy.start()

    row = lax.broadcasted_iota(jnp.int32, (tok, tok), 0)
    col = lax.broadcasted_iota(jnp.int32, (tok, tok), 1)
    within_row = lax.rem(row, half)
    query_pos = jnp.where(col < half, span_ref[2 * c], span_ref[2 * c + 1]) * half + lax.rem(col, half)
    nt = (((1,), (1,)), ((), ()))

    def block(j):
        return pl.ds(pl.multiple_of(j * tok, tok), tok)

    def scores_of(j):
        key_pos = jnp.where(row < half, span_ref[2 * j], span_ref[2 * j + 1]) * half + within_row
        visible = key_pos <= query_pos
        raw = lax.dot_general(kv[0, j], qg[0], nt, preferred_element_type=f32) * scale
        for h in range(heads):
            cols = slice(h * tok, (h + 1) * tok)
            part = jnp.where(visible, raw[:, cols], NEG)
            peak = jnp.max(part, axis=0, keepdims=True)
            weight = jnp.where(visible, jnp.exp(part - peak), 0.0)
            wts[j, :, cols] = weight
            stat[0, j, :, cols] = peak
            stat[1, j, :, cols] = jnp.sum(weight, axis=0, keepdims=True)

    def grads_of(j):
        grad = lax.dot_general(kv[1, j], qg[1], nt, preferred_element_type=f32)
        dprob[j] = grad
        stat[2, j] = jnp.sum(grad * wts[j], axis=0, keepdims=True)

    for copy in load_q:
        copy.wait()
    scores_of(c)

    def take(i):
        arrive(i).wait_recv()
        forward(i).start()

    each(n - 1, lambda i: take(i + 1))

    def use(i):
        forwarded(i).wait_recv()
        scores_of(peer(i))

    each(n - 1, lambda i: use(i + 1))
    for copy in shift:
        copy.wait_recv()
    each(n, lambda i: grads_of(peer(i)))

    peaks = stat[0]
    peak = jnp.max(peaks, axis=0, keepdims=True)
    factor = jnp.exp(peaks - peak)
    total = jnp.sum(factor * stat[1], axis=0, keepdims=True)
    factor = factor / total
    dots = jnp.sum(factor * stat[2], axis=0)
    stat[0] = factor

    share_scale = jnp.where(d == 0, scale, 1.0).astype(f32)
    other_scale = jnp.where(d == 0, 1.0, scale).astype(f32)

    def swap(i):
        j = peer(i)
        return pltpu.make_async_remote_copy(
            src_ref=xsend.at[j], dst_ref=xrecv.at[j],
            send_sem=x_send.at[j], recv_sem=x_recv.at[j],
            device_id={"dp": other}, device_id_type=MESH,
        )

    def deliver(i):
        return pltpu.make_async_remote_copy(
            src_ref=rsend.at[i], dst_ref=rrecv.at[c],
            send_sem=r_send.at[i], recv_sem=r_recv.at[c],
            device_id={"cp": peer(i)}, device_id_type=MESH,
        )

    def delivered(i):
        j = peer(i)
        return pltpu.make_async_remote_copy(
            src_ref=rsend.at[i], dst_ref=rrecv.at[j],
            send_sem=r_send.at[i], recv_sem=r_recv.at[j],
            device_id={"cp": j}, device_id_type=MESH,
        )

    def give(i):
        j = peer(i)
        prob = wts[j] * stat[0, j]
        pair[1, block(j), :] = prob.astype(bf16)
        pair[0, block(j), :] = (prob * (dprob[j] - dots)).astype(bf16)
        part = jnp.dot(pair[other, block(j), :], qg[other], preferred_element_type=f32)
        xsend[j] = (part * other_scale).astype(bf16)
        swap(i).start()

    each(n - 1, lambda i: give(i + 1))
    give(0)

    def keep(i):
        j = peer(i)
        part = jnp.dot(pair[d, block(j), :], qg[d], preferred_element_type=f32) * share_scale
        swap(i).wait_recv()
        return part + xrecv[j].astype(f32)

    def send(i):
        rsend[i] = keep(i).astype(bf16)
        deliver(i).start()

    each(n - 1, lambda i: send(i + 1))
    own[...] = keep(0)

    tn = (((0,), (0,)), ((), ()))
    keys_all = kv[0].reshape(n * tok, dh)
    values_all = kv[1].reshape(n * tok, dh)
    out_t = lax.dot_general(values_all, pair[1], tn, preferred_element_type=f32)
    for h in range(heads):
        ovm[:, h * dh:(h + 1) * dh] = out_t[:, h * tok:(h + 1) * tok].T.astype(bf16)
    put_o = pltpu.make_async_copy(ovm, o_ref.at[0], out_sem.at[0])
    put_o.start()
    dq_t = lax.dot_general(keys_all, pair[0], tn, preferred_element_type=f32) * scale
    for h in range(heads):
        dqvm[:, h * dh:(h + 1) * dh] = dq_t[:, h * tok:(h + 1) * tok].T.astype(bf16)
    put_q = pltpu.make_async_copy(dqvm, dq_ref.at[0], out_sem.at[1])
    put_q.start()

    def gather(i):
        delivered(i).wait_recv()
        own[...] += rrecv[peer(i)].astype(f32)

    each(n - 1, lambda i: gather(i + 1))
    fin[d] = own[...].astype(bf16)

    def final(share):
        return pltpu.make_async_remote_copy(
            src_ref=fin.at[share], dst_ref=fin.at[share],
            send_sem=e_send.at[0], recv_sem=e_recv.at[0],
            device_id={"dp": other}, device_id_type=MESH,
        )

    final(d).start()

    for copy in shift:
        copy.wait_send()

    def settle(i):
        spread(i).wait_send()
        forward(i).wait_send()
        deliver(i).wait_send()

    each(n - 1, lambda i: settle(i + 1))
    each(n, lambda i: swap(i).wait_send())
    final(other).wait_recv()
    put_k = pltpu.make_async_copy(fin.at[0], dk_ref.at[0], out_sem.at[2])
    put_v = pltpu.make_async_copy(fin.at[1], dv_ref.at[0], out_sem.at[3])
    put_k.start()
    put_v.start()
    final(d).wait_send()
    put_o.wait()
    put_q.wait()
    put_k.wait()
    put_v.wait()


def body(n_pp, n, n_dp, queries, keys, values, grad_out, span_order):
    tok, dh = keys.shape[1], keys.shape[2]
    heads = queries.shape[2] // dh
    width = heads * tok
    f32, bf16 = jnp.float32, jnp.bfloat16
    scratch = [
        ((2, n, tok, dh), bf16),
        ((2, width, dh), bf16),
        ((n, tok, width), f32),
        ((n, tok, width), f32),
        ((3, n, 1, width), f32),
        ((2, n * tok, width), bf16),
        ((n, tok, dh), bf16),
        ((n, tok, dh), bf16),
        ((n, tok, dh), bf16),
        ((n, tok, dh), bf16),
        ((tok, dh), f32),
        ((2, tok, dh), bf16),
        ((tok, heads * dh), bf16),
        ((tok, heads * dh), bf16),
    ]
    held = sum(math.prod(shape) * jnp.dtype(kind).itemsize for shape, kind in scratch)
    dma = pltpu.SemaphoreType.DMA
    sems = [heads, 2, 4, heads, heads, n, n, n, n, n, n, n, n, 1, 1]
    pairs = heads * tok * n * tok
    return pl.pallas_call(
        functools.partial(kernel, n_pp, n, n_dp, heads),
        out_shape=(
            jax.ShapeDtypeStruct(queries.shape, bf16),
            jax.ShapeDtypeStruct(queries.shape, bf16),
            jax.ShapeDtypeStruct(keys.shape, bf16),
            jax.ShapeDtypeStruct(values.shape, bf16),
        ),
        in_specs=[pl.BlockSpec(memory_space=pltpu.SMEM)]
        + [pl.BlockSpec(memory_space=pl.ANY)] * 4,
        out_specs=[pl.BlockSpec(memory_space=pl.ANY)] * 4,
        scratch_shapes=[pltpu.VMEM(shape, kind) for shape, kind in scratch]
        + [dma((count,)) for count in sems],
        compiler_params=pltpu.CompilerParams(
            collective_id=0,
            has_side_effects=True,
            vmem_limit_bytes=int(held * 1.25) + (8 << 20),
        ),
        cost_estimate=pl.CostEstimate(
            flops=12 * pairs * dh, bytes_accessed=8 * tok * heads * dh, transcendentals=pairs
        ),
        name="attention",
    )(span_order, queries, keys, values, grad_out)


def solution(mesh):
    in_specs = (
        P("pp", "cp", "dp"),
        P("pp", "cp", None),
        P("pp", "cp", None),
        P("pp", "cp", "dp"),
        P(),
    )
    out_specs = (P("pp", "cp", "dp"), P("pp", "cp", "dp"), P("pp", "cp", None), P("pp", "cp", None))
    sizes = [mesh.shape[axis] for axis in ("pp", "cp", "dp")]
    return jax.shard_map(
        functools.partial(body, *sizes),
        mesh=mesh, in_specs=in_specs, out_specs=out_specs, check_vma=False,
    )
```

time: 75.9 us -> 27 us (0.36)
  blocking collectives: 30.4 us -> 0 us
  Pallas kernels: 0 us -> 19.5 us
  waiting for transfers between devices: 18.4 us -> 0 us
  between operations: 14.1 us -> 0.65 us
  starting transfers between devices: 3.98 us -> 0 us
  matrix products: 2.31 us -> 0 us
  local copies, waits for them, and re-layouts: 4.79 us -> 6.51 us
  other arithmetic: 1.54 us -> 0 us
    all_gather x2 -> x0, blocking collectives: 25.9 us -> none  [the longest x1 13.6 us: body(): lax.all_gather(keys[0], 'cp', axis=0, tiled=True)]
    pallas_call x0 -> x1, Pallas kernels: none -> 19.5 us  [body(): pl.pallas_call(functools.partial(kernel, n_pp, n, n_dp, heads), out_shape...]
    reduce_scatter x1 -> x0, waiting for transfers between devices: 18.4 us -> none  [body(): lax.psum_scatter(partial_value, 'cp', scatter_dimension=0, tiled=True)]
    psum x1 -> x0, blocking collectives: 4.52 us -> none  [body(): summed = lax.psum(shared_rows, 'dp').astype(jnp.bfloat16)]
    ppermute x1 -> x0, starting transfers between devices: 3.95 us -> none  [shifted(): return lax.ppermute(block, axis, route)]
    unnamed x11 -> x14, local copies, waits for them, and re-layouts: 3.47 us -> 6.51 us
    dot_general x6 -> x0, matrix products: 2.31 us -> none  [the longest x1 0.52 us: forward_step(): jnp.einsum('thk,kd->thd', weights.astype(jnp.bfloat16), value_piece, pref...]
    another operation x1 -> x0, local copies, waits for them, and re-layouts: 1.03 us -> none  [body(): query_heads = query_rows.reshape(tok_rows, head_count, head_dim)]
  transfers between devices with their start and end apart: 2 -> 0, of which waited for: 1 -> 0; matrix products, arithmetic and copies ran while one was open for 6% -> 0% of each run, Pallas kernels for 0% -> 0%
where the time goes in v1:
time: 27 us; the launch traced here: 26.7 us
  Pallas kernels  19.5 us (72%)
  local copies, waits for them, and re-layouts  6.51 us (24%)
  between operations  0.65 us (2%)
    pallas_call x1, Pallas kernels, body(): pl.pallas_call(functools.partial(kernel, n_pp, n, n_dp, heads), out_shape...  19.5 us
    unnamed x14, local copies, waits for them, and re-layouts  6.51 us

profile of v1, /device:TPU:0, one launch (start us, length us, event | category | flops | bytes accessed | tf_op | source)
XLA Modules:
  0.0 26.7 jit_solution(15451752677258516712)
XLA Ops:
  0.6 0.0 copy-start
  0.6 0.9 %copy-done = bf16[1,128,512]{2,1,0:T(8,128)(2,1)S(1)} copy-done((bf16[1,128,512]{2,1,0:T(8,128)(2,1)S(1)}, bf16[1,128,512]{2,1,0:T(8,128)(2,1)}, u32[]{:S(2)}) %copy-start) | copy-done | bytes 131096
  1.5 0.0 copy-start.1
  1.5 0.9 %copy-done.1 = bf16[1,128,512]{2,1,0:T(8,128)(2,1)S(1)} copy-done((bf16[1,128,512]{2,1,0:T(8,128)(2,1)S(1)}, bf16[1,128,512]{2,1,0:T(8,128)(2,1)}, u32[]{:S(2)}) %copy-start.1) | copy-done | bytes 131096
  2.4 0.0 copy-start.2
  2.4 0.8 %copy-done.2 = bf16[1,128,128]{2,1,0:T(8,128)(2,1)S(1)} copy-done((bf16[1,128,128]{2,1,0:T(8,128)(2,1)S(1)}, bf16[1,128,128]{2,1,0:T(8,128)(2,1)}, u32[]{:S(2)}) %copy-start.2) | copy-done | bytes 32792
  3.2 0.0 copy-start.3
  3.2 0.8 %copy-done.3 = bf16[1,128,128]{2,1,0:T(8,128)(2,1)S(1)} copy-done((bf16[1,128,128]{2,1,0:T(8,128)(2,1)S(1)}, bf16[1,128,128]{2,1,0:T(8,128)(2,1)}, u32[]{:S(2)}) %copy-start.3) | copy-done | bytes 32792
  4.0 0.0 copy-start.4
  4.0 0.7 %copy-done.4 = s32[8]{0:T(128)S(1)} copy-done((s32[8]{0:T(128)S(1)}, s32[8]{0:T(128)}, u32[]{:S(2)}) %copy-start.4) | copy-done | bytes 56
  4.6 19.5 %attention.1 = (bf16[1,128,512]{2,1,0:T(8,128)(2,1)S(1)}, bf16[1,128,512]{2,1,0:T(8,128)(2,1)S(1)}, bf16[1,128,128]{2,1,0:T(8,128)(2,1)S(1)}, bf16[1,128,128]{2,1,0:T(8,128)(2,1)S(1)}) custom-call(s32[8]{0:T(128)S(1)} %copy-done.4, bf16[1,128,512]{2,1,0:T(8,128)(2,1)S(1)} %copy-done, bf16[1,128,128]{2,1,0:T(8,128)(2,1)S(1)} %copy-done.2, ...), custom_call_target="tpu_custom_call" | custom-call | flops 402653184 | bytes 524288 | tf_op jit(solution)/shard_map/attention/pallas_call | solution.py:304
  24.1 0.7 %copy.13 = bf16[1,128,512]{2,1,0:T(8,128)(2,1)} copy(bf16[1,128,512]{2,1,0:T(8,128)(2,1)S(1)} %get-tuple-element.8) | data formatting | bytes 262144
  24.8 0.7 %copy.14 = bf16[1,128,512]{2,1,0:T(8,128)(2,1)} copy(bf16[1,128,512]{2,1,0:T(8,128)(2,1)S(1)} %get-tuple-element.9) | data formatting | bytes 262144
  25.4 0.6 %copy.15 = bf16[1,128,128]{2,1,0:T(8,128)(2,1)} copy(bf16[1,128,128]{2,1,0:T(8,128)(2,1)S(1)} %get-tuple-element.10) | data formatting | bytes 65536
  26.1 0.6 %copy.16 = bf16[1,128,128]{2,1,0:T(8,128)(2,1)} copy(bf16[1,128,128]{2,1,0:T(8,128)(2,1)S(1)} %get-tuple-element.11) | data formatting | bytes 65536
Async XLA Ops:
  0.6 0.9 %copy-start = (bf16[1,128,512]{2,1,0:T(8,128)(2,1)S(1)}, bf16[1,128,512]{2,1,0:T(8,128)(2,1)}, u32[]{:S(2)}) copy-start(bf16[1,128,512]{2,1,0:T(8,128)(2,1)} %q_ref.1) | copy-start | bytes 393220
  1.5 0.9 %copy-start.1 = (bf16[1,128,512]{2,1,0:T(8,128)(2,1)S(1)}, bf16[1,128,512]{2,1,0:T(8,128)(2,1)}, u32[]{:S(2)}) copy-start(bf16[1,128,512]{2,1,0:T(8,128)(2,1)} %g_ref.1) | copy-start | bytes 393220
  2.4 0.8 %copy-start.2 = (bf16[1,128,128]{2,1,0:T(8,128)(2,1)S(1)}, bf16[1,128,128]{2,1,0:T(8,128)(2,1)}, u32[]{:S(2)}) copy-start(bf16[1,128,128]{2,1,0:T(8,128)(2,1)} %k_ref.1) | copy-start | bytes 98308
  3.2 0.8 %copy-start.3 = (bf16[1,128,128]{2,1,0:T(8,128)(2,1)S(1)}, bf16[1,128,128]{2,1,0:T(8,128)(2,1)}, u32[]{:S(2)}) copy-start(bf16[1,128,128]{2,1,0:T(8,128)(2,1)} %v_ref.1) | copy-start | bytes 98308
  4.0 0.7 %copy-start.4 = (s32[8]{0:T(128)S(1)}, s32[8]{0:T(128)}, u32[]{:S(2)}) copy-start(s32[8]{0:T(128)} %span_ref.1) | copy-start | bytes 100

commit v2 on v1

--- a/solution.py
+++ b/solution.py
@@ -28,13 +28,12 @@
 def kernel(
     n_pp, n, n_dp, heads, span_ref, q_ref, k_ref, v_ref, g_ref,
     o_ref, dq_ref, dk_ref, dv_ref,
-    kv, qg, wts, dprob, stat, pair, xsend, xrecv, rsend, rrecv, own, fin, ovm, dqvm,
-    q_sem, kv_sem, out_sem, g_send, g_recv, s_send, s_recv, f_send, f_recv,
+    kv, qg, wts, dprob, stat, pair, xsend, xrecv, rsend, rrecv, own, fin,
+    q_sem, kv_sem, g_send, g_recv, s_send, s_recv, f_send, f_recv,
     x_send, x_recv, r_send, r_recv, e_send, e_recv,
 ):
     tok, dh = kv.shape[2], kv.shape[3]
     half = tok // 2
-    width = heads * dh if False else heads * tok
     scale = 1.0 / math.sqrt(dh)
     f32, bf16 = jnp.float32, jnp.bfloat16
     s = lax.axis_index("pp")
@@ -229,14 +228,10 @@
     values_all = kv[1].reshape(n * tok, dh)
     out_t = lax.dot_general(values_all, pair[1], tn, preferred_element_type=f32)
     for h in range(heads):
-        ovm[:, h * dh:(h + 1) * dh] = out_t[:, h * tok:(h + 1) * tok].T.astype(bf16)
-    put_o = pltpu.make_async_copy(ovm, o_ref.at[0], out_sem.at[0])
-    put_o.start()
+        o_ref[0, :, h * dh:(h + 1) * dh] = out_t[:, h * tok:(h + 1) * tok].T.astype(bf16)
     dq_t = lax.dot_general(keys_all, pair[0], tn, preferred_element_type=f32) * scale
     for h in range(heads):
-        dqvm[:, h * dh:(h + 1) * dh] = dq_t[:, h * tok:(h + 1) * tok].T.astype(bf16)
-    put_q = pltpu.make_async_copy(dqvm, dq_ref.at[0], out_sem.at[1])
-    put_q.start()
+        dq_ref[0, :, h * dh:(h + 1) * dh] = dq_t[:, h * tok:(h + 1) * tok].T.astype(bf16)
 
     def gather(i):
         delivered(i).wait_recv()
@@ -265,15 +260,21 @@
     each(n - 1, lambda i: settle(i + 1))
     each(n, lambda i: swap(i).wait_send())
     final(other).wait_recv()
-    put_k = pltpu.make_async_copy(fin.at[0], dk_ref.at[0], out_sem.at[2])
-    put_v = pltpu.make_async_copy(fin.at[1], dv_ref.at[0], out_sem.at[3])
-    put_k.start()
-    put_v.start()
+    dk_ref[0] = fin[0]
+    dv_ref[0] = fin[1]
     final(d).wait_send()
-    put_o.wait()
-    put_q.wait()
-    put_k.wait()
-    put_v.wait()
+
+
+def writer(*refs):
+    count = len(refs) // 2
+    sem = refs[-1]
+    copies = [
+        pltpu.make_async_copy(refs[i], refs[count + i], sem.at[i]) for i in range(count)
+    ]
+    for copy in copies:
+        copy.start()
+    for copy in copies:
+        copy.wait()
 
 
 def body(n_pp, n, n_dp, queries, keys, values, grad_out, span_order):
@@ -294,36 +295,43 @@
         ((n, tok, dh), bf16),
         ((tok, dh), f32),
         ((2, tok, dh), bf16),
-        ((tok, heads * dh), bf16),
-        ((tok, heads * dh), bf16),
     ]
     held = sum(math.prod(shape) * jnp.dtype(kind).itemsize for shape, kind in scratch)
     dma = pltpu.SemaphoreType.DMA
-    sems = [heads, 2, 4, heads, heads, n, n, n, n, n, n, n, n, 1, 1]
+    sems = [heads, 2, heads, heads, n, n, n, n, n, n, n, n, 1, 1]
     pairs = heads * tok * n * tok
-    return pl.pallas_call(
+    results = pl.pallas_call(
         functools.partial(kernel, n_pp, n, n_dp, heads),
         out_shape=(
-            jax.ShapeDtypeStruct(queries.shape, bf16),
-            jax.ShapeDtypeStruct(queries.shape, bf16),
-            jax.ShapeDtypeStruct(keys.shape, bf16),
-            jax.ShapeDtypeStruct(values.shape, bf16),
+            pltpu.VMEM(queries.shape, bf16),
+            pltpu.VMEM(queries.shape, bf16),
+            pltpu.VMEM(keys.shape, bf16),
+            pltpu.VMEM(values.shape, bf16),
         ),
         in_specs=[pl.BlockSpec(memory_space=pltpu.SMEM)]
-        + [pl.BlockSpec(memory_space=pl.ANY)] * 4,
-        out_specs=[pl.BlockSpec(memory_space=pl.ANY)] * 4,
+        + [pl.BlockSpec(memory_space=pltpu.HBM)] * 4,
+        out_specs=[pl.BlockSpec(memory_space=pltpu.VMEM)] * 4,
         scratch_shapes=[pltpu.VMEM(shape, kind) for shape, kind in scratch]
         + [dma((count,)) for count in sems],
         compiler_params=pltpu.CompilerParams(
             collective_id=0,
             has_side_effects=True,
-            vmem_limit_bytes=int(held * 1.25) + (8 << 20),
+            vmem_limit_bytes=60 << 20,
         ),
         cost_estimate=pl.CostEstimate(
             flops=12 * pairs * dh, bytes_accessed=8 * tok * heads * dh, transcendentals=pairs
         ),
         name="attention",
     )(span_order, queries, keys, values, grad_out)
+    return pl.pallas_call(
+        writer,
+        out_shape=[jax.ShapeDtypeStruct(r.shape, r.dtype) for r in results],
+        in_specs=[pl.BlockSpec(memory_space=pl.ANY)] * 4,
+        out_specs=[pl.BlockSpec(memory_space=pltpu.HBM)] * 4,
+        scratch_shapes=[dma((4,))],
+        compiler_params=pltpu.CompilerParams(vmem_limit_bytes=4 << 20),
+        name="writer",
+    )(*results)
 
 
 def solution(mesh):

time: 27 us -> 21.2 us (0.79)
  local copies, waits for them, and re-layouts: 6.51 us -> 0 us
  Pallas kernels: 19.5 us -> 20.4 us
    unnamed x14 -> x0, local copies, waits for them, and re-layouts: 6.51 us -> none
    pallas_call x0 -> x1, Pallas kernels: none -> 0.75 us  [body(): pl.pallas_call(writer, out_shape=[jax.ShapeDtypeStruct(r.shape, r.dtype)...]
where the time goes in v2:
time: 21.2 us; the launch traced here: 21 us
  Pallas kernels  20.4 us (96%)
  between operations  0.64 us (3%)
    pallas_call x1, Pallas kernels, body(): pl.pallas_call(functools.partial(kernel, n_pp, n, n_dp, heads), out_shape...  19.6 us
    pallas_call x1, Pallas kernels, body(): pl.pallas_call(writer, out_shape=[jax.ShapeDtypeStruct(r.shape, r.dtype)...  0.75 us

profile of v2, /device:TPU:0, one launch (start us, length us, event | category | flops | bytes accessed | tf_op | source)
XLA Modules:
  0.0 21.0 jit_solution(14281248105722138873)
XLA Ops:
  0.6 19.6 %attention.1 = (bf16[1,128,512]{2,1,0:T(8,128)(2,1)S(1)}, bf16[1,128,512]{2,1,0:T(8,128)(2,1)S(1)}, bf16[1,128,128]{2,1,0:T(8,128)(2,1)S(1)}, bf16[1,128,128]{2,1,0:T(8,128)(2,1)S(1)}) custom-call(s32[8]{0:T(128)} %span_ref.1, bf16[1,128,512]{2,1,0:T(8,128)(2,1)} %q_ref.1, bf16[1,128,128]{2,1,0:T(8,128)(2,1)} %k_ref.1, bf16[1,128,128]{2,1,0:T(8,128)(2,1)} %v_ref.1, ...), custom_call_target="tpu_custom_call" | custom-call | flops 402653184 | bytes 524288 | tf_op jit(solution)/shard_map/attention/pallas_call | solution.py:303
  20.2 0.7 %writer.1 = (bf16[1,128,512]{2,1,0:T(8,128)(2,1)}, bf16[1,128,512]{2,1,0:T(8,128)(2,1)}, bf16[1,128,128]{2,1,0:T(8,128)(2,1)}, bf16[1,128,128]{2,1,0:T(8,128)(2,1)}) custom-call(bf16[1,128,512]{2,1,0:T(8,128)(2,1)S(1)} %get-tuple-element.8.refs_0_, bf16[1,128,512]{2,1,0:T(8,128)(2,1)S(1)} %get-tuple-element.9.refs_1_, ...), custom_call_target="tpu_custom_call" | custom-call | tf_op jit(solution)/shard_map/writer/pallas_call | solution.py:326

commit v3 on v2

--- a/solution.py
+++ b/solution.py
@@ -43,19 +43,26 @@
     before = lax.rem(s + n_pp - 1, n_pp)
     after = lax.rem(s + 1, n_pp)
 
-    def peer(i):
-        return lax.rem(c + i, n)
+    def rising(i):
+        return i - 1 + (i - 1 - c + n) // n
+
+    def falling(i):
+        return rising(n - i)
+
+    def nearing(i):
+        wrapped = (c + i) // n
+        return (1 - wrapped) * (c + i) + wrapped * (n - 1 - i)
 
     barrier = pltpu.get_barrier_semaphore()
+    each(
+        n - 1,
+        lambda i: pl.semaphore_signal(
+            barrier, inc=1, device_id={"cp": rising(i + 1)}, device_id_type=MESH
+        ),
+    )
     pl.semaphore_signal(barrier, inc=1, device_id={"pp": before}, device_id_type=MESH)
     pl.semaphore_signal(barrier, inc=1, device_id={"pp": after}, device_id_type=MESH)
     pl.semaphore_signal(barrier, inc=1, device_id={"dp": other}, device_id_type=MESH)
-    each(
-        n - 1,
-        lambda i: pl.semaphore_signal(
-            barrier, inc=1, device_id={"cp": peer(i + 1)}, device_id_type=MESH
-        ),
-    )
 
     load_k = pltpu.make_async_copy(k_ref.at[0], kv.at[0, c], kv_sem.at[0])
     load_v = pltpu.make_async_copy(v_ref.at[0], kv.at[1, c], kv_sem.at[1])
@@ -74,38 +81,35 @@
 
     pl.semaphore_wait(barrier, n + 2)
 
-    def spread(i):
+    def spread(j):
         return pltpu.make_async_remote_copy(
             src_ref=kv.at[d, c], dst_ref=kv.at[d, c],
-            send_sem=s_send.at[i], recv_sem=s_recv.at[c],
-            device_id={"cp": peer(i)}, device_id_type=MESH,
-        )
-
-    def arrive(i):
-        j = peer(i)
+            send_sem=s_send.at[j], recv_sem=s_recv.at[c],
+            device_id={"cp": j}, device_id_type=MESH,
+        )
+
+    def arrive(j):
         return pltpu.make_async_remote_copy(
             src_ref=kv.at[d, j], dst_ref=kv.at[d, j],
-            send_sem=s_send.at[i], recv_sem=s_recv.at[j],
+            send_sem=s_send.at[j], recv_sem=s_recv.at[j],
             device_id={"cp": j}, device_id_type=MESH,
         )
 
-    def forward(i):
-        j = peer(i)
+    def forward(j):
         return pltpu.make_async_remote_copy(
             src_ref=kv.at[d, j], dst_ref=kv.at[d, j],
-            send_sem=f_send.at[i], recv_sem=f_recv.at[j],
+            send_sem=f_send.at[j], recv_sem=f_recv.at[j],
             device_id={"dp": other}, device_id_type=MESH,
         )
 
-    def forwarded(i):
-        j = peer(i)
+    def forwarded(j):
         return pltpu.make_async_remote_copy(
             src_ref=kv.at[other, j], dst_ref=kv.at[other, j],
-            send_sem=f_send.at[i], recv_sem=f_recv.at[j],
+            send_sem=f_send.at[j], recv_sem=f_recv.at[j],
             device_id={"dp": other}, device_id_type=MESH,
         )
 
-    each(n - 1, lambda i: spread(i + 1).start())
+    each(n - 1, lambda i: spread(falling(i + 1)).start())
     shift = [
         pltpu.make_async_remote_copy(
             src_ref=g_ref.at[0, :, pl.ds(h * dh, dh)],
@@ -150,19 +154,25 @@
     scores_of(c)
 
     def take(i):
-        arrive(i).wait_recv()
-        forward(i).start()
-
-    each(n - 1, lambda i: take(i + 1))
+        arrive(nearing(i)).wait_recv()
+        forward(nearing(i)).start()
 
     def use(i):
-        forwarded(i).wait_recv()
-        scores_of(peer(i))
-
-    each(n - 1, lambda i: use(i + 1))
+        forwarded(nearing(i)).wait_recv()
+        scores_of(nearing(i))
+
+    def take_and_use(i):
+        take(i + 2)
+        use(i + 1)
+
+    take(1)
+    each(n - 2, take_and_use)
     for copy in shift:
         copy.wait_recv()
-    each(n, lambda i: grads_of(peer(i)))
+    grads_of(c)
+    each(n - 2, lambda i: grads_of(nearing(i + 1)))
+    use(n - 1)
+    grads_of(nearing(n - 1))
 
     peaks = stat[0]
     peak = jnp.max(peaks, axis=0, keepdims=True)
@@ -175,53 +185,49 @@
     share_scale = jnp.where(d == 0, scale, 1.0).astype(f32)
     other_scale = jnp.where(d == 0, 1.0, scale).astype(f32)
 
-    def swap(i):
-        j = peer(i)
+    def swap(j):
         return pltpu.make_async_remote_copy(
             src_ref=xsend.at[j], dst_ref=xrecv.at[j],
             send_sem=x_send.at[j], recv_sem=x_recv.at[j],
             device_id={"dp": other}, device_id_type=MESH,
         )
 
-    def deliver(i):
-        return pltpu.make_async_remote_copy(
-            src_ref=rsend.at[i], dst_ref=rrecv.at[c],
-            send_sem=r_send.at[i], recv_sem=r_recv.at[c],
-            device_id={"cp": peer(i)}, device_id_type=MESH,
-        )
-
-    def delivered(i):
-        j = peer(i)
-        return pltpu.make_async_remote_copy(
-            src_ref=rsend.at[i], dst_ref=rrecv.at[j],
-            send_sem=r_send.at[i], recv_sem=r_recv.at[j],
+    def deliver(j):
+        return pltpu.make_async_remote_copy(
+            src_ref=rsend.at[j], dst_ref=rrecv.at[c],
+            send_sem=r_send.at[j], recv_sem=r_recv.at[c],
             device_id={"cp": j}, device_id_type=MESH,
         )
 
-    def give(i):
-        j = peer(i)
+    def delivered(j):
+        return pltpu.make_async_remote_copy(
+            src_ref=rsend.at[j], dst_ref=rrecv.at[j],
+            send_sem=r_send.at[j], recv_sem=r_recv.at[j],
+            device_id={"cp": j}, device_id_type=MESH,
+        )
+
+    def give(j):
         prob = wts[j] * stat[0, j]
         pair[1, block(j), :] = prob.astype(bf16)
         pair[0, block(j), :] = (prob * (dprob[j] - dots)).astype(bf16)
         part = jnp.dot(pair[other, block(j), :], qg[other], preferred_element_type=f32)
         xsend[j] = (part * other_scale).astype(bf16)
-        swap(i).start()
-
-    each(n - 1, lambda i: give(i + 1))
-    give(0)
-
-    def keep(i):
-        j = peer(i)
+        swap(j).start()
+
+    each(n - 1, lambda i: give(rising(i + 1)))
+    give(c)
+
+    def keep(j):
         part = jnp.dot(pair[d, block(j), :], qg[d], preferred_element_type=f32) * share_scale
-        swap(i).wait_recv()
+        swap(j).wait_recv()
         return part + xrecv[j].astype(f32)
 
-    def send(i):
-        rsend[i] = keep(i).astype(bf16)
-        deliver(i).start()
-
-    each(n - 1, lambda i: send(i + 1))
-    own[...] = keep(0)
+    def send(j):
+        rsend[j] = keep(j).astype(bf16)
+        deliver(j).start()
+
+    each(n - 1, lambda i: send(rising(i + 1)))
+    own[...] = keep(c)
 
     tn = (((0,), (0,)), ((), ()))
     keys_all = kv[0].reshape(n * tok, dh)
@@ -233,11 +239,11 @@
     for h in range(heads):
         dq_ref[0, :, h * dh:(h + 1) * dh] = dq_t[:, h * tok:(h + 1) * tok].T.astype(bf16)
 
-    def gather(i):
-        delivered(i).wait_recv()
-        own[...] += rrecv[peer(i)].astype(f32)
-
-    each(n - 1, lambda i: gather(i + 1))
+    def gather(j):
+        delivered(j).wait_recv()
+        own[...] += rrecv[j].astype(f32)
+
+    each(n - 1, lambda i: gather(rising(i + 1)))
     fin[d] = own[...].astype(bf16)
 
     def final(share):
@@ -252,13 +258,13 @@
     for copy in shift:
         copy.wait_send()
 
-    def settle(i):
-        spread(i).wait_send()
-        forward(i).wait_send()
-        deliver(i).wait_send()
-
-    each(n - 1, lambda i: settle(i + 1))
-    each(n, lambda i: swap(i).wait_send())
+    def settle(j):
+        spread(j).wait_send()
+        forward(j).wait_send()
+        deliver(j).wait_send()
+
+    each(n - 1, lambda i: settle(rising(i + 1)))
+    each(n, lambda j: swap(j).wait_send())
     final(other).wait_recv()
     dk_ref[0] = fin[0]
     dv_ref[0] = fin[1]

time: 21.2 us -> 20.6 us (0.972)
  Pallas kernels: 20.4 us -> 19.8 us
    pallas_call x1, Pallas kernels: 19.6 us -> 19 us  [body(): pl.pallas_call(functools.partial(kernel, n_pp, n, n_dp, heads), out_shape...]
where the time goes in v3:
time: 20.6 us; the launch traced here: 20.4 us
  Pallas kernels  19.8 us (96%)
  between operations  0.64 us (3%)
    pallas_call x1, Pallas kernels, body(): pl.pallas_call(functools.partial(kernel, n_pp, n, n_dp, heads), out_shape...  19 us
    pallas_call x1, Pallas kernels, body(): pl.pallas_call(writer, out_shape=[jax.ShapeDtypeStruct(r.shape, r.dtype)...  0.75 us

profile of v3, /device:TPU:0, one launch (start us, length us, event | category | flops | bytes accessed | tf_op | source)
XLA Modules:
  0.0 20.4 jit_solution(625639371634476259)
XLA Ops:
  0.6 19.0 %attention.1 = (bf16[1,128,512]{2,1,0:T(8,128)(2,1)S(1)}, bf16[1,128,512]{2,1,0:T(8,128)(2,1)S(1)}, bf16[1,128,128]{2,1,0:T(8,128)(2,1)S(1)}, bf16[1,128,128]{2,1,0:T(8,128)(2,1)S(1)}) custom-call(s32[8]{0:T(128)} %span_ref.1, bf16[1,128,512]{2,1,0:T(8,128)(2,1)} %q_ref.1, bf16[1,128,128]{2,1,0:T(8,128)(2,1)} %k_ref.1, bf16[1,128,128]{2,1,0:T(8,128)(2,1)} %v_ref.1, ...), custom_call_target="tpu_custom_call" | custom-call | flops 402653184 | bytes 524288 | tf_op jit(solution)/shard_map/attention/pallas_call | solution.py:309
  19.7 0.7 %writer.1 = (bf16[1,128,512]{2,1,0:T(8,128)(2,1)}, bf16[1,128,512]{2,1,0:T(8,128)(2,1)}, bf16[1,128,128]{2,1,0:T(8,128)(2,1)}, bf16[1,128,128]{2,1,0:T(8,128)(2,1)}) custom-call(bf16[1,128,512]{2,1,0:T(8,128)(2,1)S(1)} %get-tuple-element.8.refs_0_, bf16[1,128,512]{2,1,0:T(8,128)(2,1)S(1)} %get-tuple-element.9.refs_1_, ...), custom_call_target="tpu_custom_call" | custom-call | tf_op jit(solution)/shard_map/writer/pallas_call | solution.py:332

commit v4 on v3

--- a/solution.py
+++ b/solution.py
@@ -26,10 +26,10 @@
 
 
 def kernel(
-    n_pp, n, n_dp, heads, span_ref, q_ref, k_ref, v_ref, g_ref,
+    n_pp, n, n_dp, heads, span_hbm, q_ref, k_ref, v_ref, g_ref,
     o_ref, dq_ref, dk_ref, dv_ref,
-    kv, qg, wts, dprob, stat, pair, xsend, xrecv, rsend, rrecv, own, fin,
-    q_sem, kv_sem, g_send, g_recv, s_send, s_recv, f_send, f_recv,
+    kv, qg, wts, dprob, stat, pair, xsend, xrecv, rsend, rrecv, own, fin, span_ref,
+    span_sem, q_sem, kv_sem, g_send, g_recv, s_send, s_recv, f_send, f_recv,
     x_send, x_recv, r_send, r_recv, e_send, e_recv,
 ):
     tok, dh = kv.shape[2], kv.shape[3]
@@ -60,7 +60,6 @@
             barrier, inc=1, device_id={"cp": rising(i + 1)}, device_id_type=MESH
         ),
     )
-    pl.semaphore_signal(barrier, inc=1, device_id={"pp": before}, device_id_type=MESH)
     pl.semaphore_signal(barrier, inc=1, device_id={"pp": after}, device_id_type=MESH)
     pl.semaphore_signal(barrier, inc=1, device_id={"dp": other}, device_id_type=MESH)
 
@@ -76,10 +75,12 @@
     ]
     for copy in load_q:
         copy.start()
+    load_span = pltpu.make_async_copy(span_hbm, span_ref, span_sem.at[0])
+    load_span.start()
     load_k.wait()
     load_v.wait()
 
-    pl.semaphore_wait(barrier, n + 2)
+    pl.semaphore_wait(barrier, n + 1)
 
     def spread(j):
         return pltpu.make_async_remote_copy(
@@ -122,6 +123,7 @@
     for copy in shift:
         copy.start()
 
+    load_span.wait()
     row = lax.broadcasted_iota(jnp.int32, (tok, tok), 0)
     col = lax.broadcasted_iota(jnp.int32, (tok, tok), 1)
     within_row = lax.rem(row, half)
@@ -165,8 +167,8 @@
         take(i + 2)
         use(i + 1)
 
-    take(1)
-    each(n - 2, take_and_use)
+    each(n - 1, lambda i: take(i + 1))
+    each(n - 2, lambda i: use(i + 1))
     for copy in shift:
         copy.wait_recv()
     grads_of(c)
@@ -304,7 +306,7 @@
     ]
     held = sum(math.prod(shape) * jnp.dtype(kind).itemsize for shape, kind in scratch)
     dma = pltpu.SemaphoreType.DMA
-    sems = [heads, 2, heads, heads, n, n, n, n, n, n, n, n, 1, 1]
+    sems = [1, heads, 2, heads, heads, n, n, n, n, n, n, n, n, 1, 1]
     pairs = heads * tok * n * tok
     results = pl.pallas_call(
         functools.partial(kernel, n_pp, n, n_dp, heads),
@@ -314,10 +316,10 @@
             pltpu.VMEM(keys.shape, bf16),
             pltpu.VMEM(values.shape, bf16),
         ),
-        in_specs=[pl.BlockSpec(memory_space=pltpu.SMEM)]
-        + [pl.BlockSpec(memory_space=pltpu.HBM)] * 4,
+        in_specs=[pl.BlockSpec(memory_space=pltpu.HBM)] * 5,
         out_specs=[pl.BlockSpec(memory_space=pltpu.VMEM)] * 4,
         scratch_shapes=[pltpu.VMEM(shape, kind) for shape, kind in scratch]
+        + [pltpu.SMEM(span_order.shape, jnp.int32)]
         + [dma((count,)) for count in sems],
         compiler_params=pltpu.CompilerParams(
             collective_id=0,

time: 20.6 us -> 19.5 us (0.947)
  Pallas kernels: 19.8 us -> 18.6 us
    pallas_call x1, Pallas kernels: 19 us -> 17.9 us  [body(): pl.pallas_call(functools.partial(kernel, n_pp, n, n_dp, heads), out_shape...]
where the time goes in v4:
time: 19.5 us; the launch traced here: 19.3 us
  Pallas kernels  18.6 us (95%)
  between operations  0.64 us (3%)
    pallas_call x1, Pallas kernels, body(): pl.pallas_call(functools.partial(kernel, n_pp, n, n_dp, heads), out_shape...  17.9 us
    pallas_call x1, Pallas kernels, body(): pl.pallas_call(writer, out_shape=[jax.ShapeDtypeStruct(r.shape, r.dtype)...  0.75 us

profile of v4, /device:TPU:0, one launch (start us, length us, event | category | flops | bytes accessed | tf_op | source)
XLA Modules:
  0.0 19.3 jit_solution(3806772987484415841)
XLA Ops:
  0.6 17.9 %attention.1 = (bf16[1,128,512]{2,1,0:T(8,128)(2,1)S(1)}, bf16[1,128,512]{2,1,0:T(8,128)(2,1)S(1)}, bf16[1,128,128]{2,1,0:T(8,128)(2,1)S(1)}, bf16[1,128,128]{2,1,0:T(8,128)(2,1)S(1)}) custom-call(s32[8]{0:T(128)} %span_hbm.1, bf16[1,128,512]{2,1,0:T(8,128)(2,1)} %q_ref.1, bf16[1,128,128]{2,1,0:T(8,128)(2,1)} %k_ref.1, bf16[1,128,128]{2,1,0:T(8,128)(2,1)} %v_ref.1, ...), custom_call_target="tpu_custom_call" | custom-call | flops 402653184 | bytes 524288 | tf_op jit(solution)/shard_map/attention/pallas_call | solution.py:311
  18.5 0.7 %writer.1 = (bf16[1,128,512]{2,1,0:T(8,128)(2,1)}, bf16[1,128,512]{2,1,0:T(8,128)(2,1)}, bf16[1,128,128]{2,1,0:T(8,128)(2,1)}, bf16[1,128,128]{2,1,0:T(8,128)(2,1)}) custom-call(bf16[1,128,512]{2,1,0:T(8,128)(2,1)S(1)} %get-tuple-element.8.refs_0_, bf16[1,128,512]{2,1,0:T(8,128)(2,1)S(1)} %get-tuple-element.9.refs_1_, ...), custom_call_target="tpu_custom_call" | custom-call | tf_op jit(solution)/shard_map/writer/pallas_call | solution.py:334

commit v5 on v4

--- a/solution.py
+++ b/solution.py
@@ -216,8 +216,6 @@
         xsend[j] = (part * other_scale).astype(bf16)
         swap(j).start()
 
-    each(n - 1, lambda i: give(rising(i + 1)))
-    give(c)
 
     def keep(j):
         part = jnp.dot(pair[d, block(j), :], qg[d], preferred_element_type=f32) * share_scale
@@ -228,7 +226,10 @@
         rsend[j] = keep(j).astype(bf16)
         deliver(j).start()
 
-    each(n - 1, lambda i: send(rising(i + 1)))
+    each(n - 1, lambda i: give(rising(i + 1)))
+    send(rising(1))
+    give(c)
+    each(n - 2, lambda i: send(rising(i + 2)))
     own[...] = keep(c)
 
     tn = (((0,), (0,)), ((), ()))

time: 19.5 us -> 19.4 us (level)
  no operation moved by 1% of the time
where the time goes in v5:
time: 19.4 us; the launch traced here: 19.2 us
  Pallas kernels  18.5 us (95%)
  between operations  0.64 us (3%)
    pallas_call x1, Pallas kernels, body(): pl.pallas_call(functools.partial(kernel, n_pp, n, n_dp, heads), out_shape...  17.8 us
    pallas_call x1, Pallas kernels, body(): pl.pallas_call(writer, out_shape=[jax.ShapeDtypeStruct(r.shape, r.dtype)...  0.75 us

profile of v5, /device:TPU:0, one launch (start us, length us, event | category | flops | bytes accessed | tf_op | source)
XLA Modules:
  0.0 19.2 jit_solution(871068683871915322)
XLA Ops:
  0.6 17.8 %attention.1 = (bf16[1,128,512]{2,1,0:T(8,128)(2,1)S(1)}, bf16[1,128,512]{2,1,0:T(8,128)(2,1)S(1)}, bf16[1,128,128]{2,1,0:T(8,128)(2,1)S(1)}, bf16[1,128,128]{2,1,0:T(8,128)(2,1)S(1)}) custom-call(s32[8]{0:T(128)} %span_hbm.1, bf16[1,128,512]{2,1,0:T(8,128)(2,1)} %q_ref.1, bf16[1,128,128]{2,1,0:T(8,128)(2,1)} %k_ref.1, bf16[1,128,128]{2,1,0:T(8,128)(2,1)} %v_ref.1, ...), custom_call_target="tpu_custom_call" | custom-call | flops 402653184 | bytes 524288 | tf_op jit(solution)/shard_map/attention/pallas_call | solution.py:312
  18.4 0.7 %writer.1 = (bf16[1,128,512]{2,1,0:T(8,128)(2,1)}, bf16[1,128,512]{2,1,0:T(8,128)(2,1)}, bf16[1,128,128]{2,1,0:T(8,128)(2,1)}, bf16[1,128,128]{2,1,0:T(8,128)(2,1)}) custom-call(bf16[1,128,512]{2,1,0:T(8,128)(2,1)S(1)} %get-tuple-element.8.refs_0_, bf16[1,128,512]{2,1,0:T(8,128)(2,1)S(1)} %get-tuple-element.9.refs_1_, ...), custom_call_target="tpu_custom_call" | custom-call | tf_op jit(solution)/shard_map/writer/pallas_call | solution.py:335
